TPU v7x, 32 devices: a whole 2x2x4 slice. The times are simulated.
32 devices in a mesh: rep: 4 (over y, x), fsdp: 8 (over z, core).
Axes of the slice: x: 2, y: 2, z: 4, core: 2. Of those that a mesh axis runs over, the one named last changes fastest.
Arguments:
- accumulated: bfloat16 [4, 1024, 14336], P('rep', 'fsdp'), may hold values from -48 to 48
- start_q: bfloat16 [32, 14336], replicated, may hold values from -6 to 6
- max_rms: float32 [1], replicated, as said below
Outputs:
- update: bfloat16 [1024, 14336], P('fsdp', 'rep')
- next_q: float32 [32, 14336], P(None, ('rep', 'fsdp'))
Inputs may be any that keep to these rules, and one draw needn't show every extreme that they name: `max_rms`: a positive threshold.
All inputs are finite; a program needn't handle non-finite values.
Results may differ from a plain program's by a relative error of at most 0.0064.
Values may be sent and summed in bfloat16 or wider, within the bound.
A program may use at most 64 MiB of HBM per device.

v0:
```python
import math

import jax
import jax.numpy as jnp
from jax import lax
from jax.sharding import PartitionSpec as P


def orthonormal(part_rows, gram):
    lower = jnp.linalg.cholesky(gram)
    return lax.linalg.triangular_solve(
        lower, part_rows, left_side=False, lower=True, transpose_a=True
    )


def on_device(accumulated, start_q, max_rms):
    shard = accumulated[0]
    rows = shard.shape[0]
    width = shard.shape[1]
    n_rep = lax.axis_size("rep")
    n_fsdp = lax.axis_size("fsdp")
    total_rows = rows * n_fsdp
    local_p = lax.dot_general(
        shard, start_q, (((1,), (1,)), ((), ())), preferred_element_type=jnp.float32
    )
    p_sum = lax.psum(local_p, "rep")
    gram = lax.psum(jnp.dot(p_sum.T, p_sum, precision=lax.Precision.HIGHEST), "fsdp")
    p_round = orthonormal(p_sum, gram).astype(jnp.bfloat16)
    block_cols = width // n_rep
    own_cols = width // (n_rep * n_fsdp)
    q_full = lax.psum(
        lax.dot_general(
            p_round, shard, (((0,), (0,)), ((), ())), preferred_element_type=jnp.float32
        ),
        ("rep", "fsdp"),
    )
    norm_sq = jnp.sum(q_full * q_full)
    q_block = lax.dynamic_slice_in_dim(
        q_full, lax.axis_index("rep") * block_cols, block_cols, 1
    ).astype(jnp.bfloat16)
    product = jnp.dot(p_round, q_block, preferred_element_type=jnp.float32)
    next_q = lax.dynamic_slice_in_dim(
        q_full, lax.axis_index(("rep", "fsdp")) * own_cols, own_cols, 1
    )
    scale = jnp.minimum(1.0, max_rms[0] * math.sqrt(total_rows * width) / jnp.sqrt(norm_sq))
    update = (scale * product).astype(jnp.bfloat16)
    return (update, next_q)


def solution(mesh):
    return jax.shard_map(
        on_device,
        mesh=mesh,
        in_specs=(P("rep", "fsdp", None), P(), P()),
        out_specs=(P("fsdp", "rep"), P(None, ("rep", "fsdp"))),
        check_vma=False,
    )
```

profile of v0, /device:TPU:0, one launch (start us, length us, event | category | flops | bytes accessed | tf_op | source)
XLA Modules:
  0.0 209.7 jit_solution(9343352515493051389)
XLA Ops:
  7.2 0.0 copy-start
  7.2 0.0 all-reduce.2.cloned.1.call-start
  7.2 1.1 copy-done
  8.3 3.4 %fusion.3 = f32[128,32]{0,1:T(8,128)S(1)} fusion(bf16[32,14336]{1,0:T(8,128)(2,1)S(1)} %copy-done, bf16[1,128,14336]{2,1,0:T(8,128)(2,1)} %param.3), kind=kOutput, calls=%fused_computation.4 | convolution fusion | flops 117440512 | bytes 4603904 | tf_op jit(solution)/shard_map/dot_general | solution.py:23
  11.7 17.5 %psum.21 = f32[128,32]{0,1:T(8,128)S(1)} all-reduce(f32[128,32]{0,1:T(8,128)S(1)} %fusion.3), channel_id=1, replica_groups=mesh['rep'=4,'fsdp'=8] {'rep'}, use_global_device_ids=true, to_apply=%region_0.0 | all-reduce | flops 4096 | bytes 32768 | tf_op jit(solution)/shard_map/psum | solution.py:26
  29.2 0.1 fusion.9
  29.4 26.0 %psum.22 = f32[32,32]{0,1:T(8,128)S(1)} all-reduce(f32[32,32]{0,1:T(8,128)S(1)} %fusion.9), channel_id=1, replica_groups=mesh['rep'=4,'fsdp'=8] {'fsdp'}, use_global_device_ids=true, to_apply=%region_1.0 | all-reduce | flops 1024 | bytes 8192 | tf_op jit(solution)/shard_map/psum | solution.py:27
  55.3 0.1 copy.6
  55.4 2.9 %cholesky.16 = f32[32,32]{1,0:T(8,128)S(1)} custom-call(f32[32,32]{1,0:T(8,128)S(1)} %fusion.7), custom_call_target="Cholesky" | custom-call | tf_op jit(solution)/shard_map/jit(cholesky)/cholesky | solution.py:10
  58.4 0.6 compare_reduce_fusion
  59.0 0.7 fusion.5
  59.7 2.5 %custom-call.6 = f32[1,32,32]{1,2,0:T(8,128)S(1)} custom-call(f32[1,32,32]{2,1,0:T(8,128)S(1)} %fusion.5), custom_call_target="InvertDiagBlocksLowerTriangular" | custom-call | tf_op jit(solution)/shard_map/triangular_solve | solution.py:11
  62.1 0.2 convolution_convert_fusion
  62.4 3.9 %fusion.1 = f32[32,14336]{1,0:T(8,128)} fusion(bf16[128,32]{0,1:T(8,128)(2,1)S(1)} %convolution_convert_fusion, bf16[1,128,14336]{2,1,0:T(8,128)(2,1)} %param.3), kind=kOutput, calls=%fused_computation.2 | convolution fusion | flops 117440512 | bytes 5513216 | tf_op jit(solution)/shard_map/dot_general | solution.py:32
  66.2 0.0 all-reduce.2.cloned.1.call-update
  66.9 128.7 %all-reduce.2.cloned.1.call-done = f32[32,14336]{1,0:T(8,128)} async-done(((f32[32,14336]{1,0:T(8,128)}), f32[32,14336]{1,0:T(8,128)}) %all-reduce.2.cloned.1.call-update) | async-done | bytes 1835024 | tf_op jit(solution)/shard_map/psum | solution.py:31
  195.7 2.6 %multiply_reduce_fusion = f32[]{:T(128)} fusion(f32[32,14336]{1,0:T(8,128)} %all-reduce.2.cloned.1.call-done), kind=kLoop, calls=%fused_computation.6 | loop fusion | flops 917503 | bytes 1835012 | tf_op jit(solution)/shard_map/reduce_sum | solution.py:37
  198.9 1.6 constant_dynamic-slice_fusion
  200.5 2.4 %fusion = bf16[128,3584]{1,0:T(8,128)(2,1)} fusion(bf16[128,32]{0,1:T(8,128)(2,1)S(1)} %convolution_convert_fusion, f32[]{:T(128)S(6)} %min_shard_map.3, f32[32,14336]{1,0:T(8,128)} %all-reduce.2.cloned.1.call-done, s32[]{:T(128)S(6)} %select_n.11), kind=kOutput, calls=%fused_computation.1 | convolution fusion | flops 30277632 | bytes 1155080 | tf_op jit(solution)/shard_map/dot_general | solution.py:41
  (2 shorter events, 0.0 us)
Async XLA Ops:
  7.2 1.2 copy-start
  7.2 188.5 %all-reduce.2.cloned.1.call-start = ((), (), s32[]{:S(2)}) async-start(), calls=%async_computation | async-start | bytes 3670016 | tf_op jit(solution)/shard_map/psum | solution.py:31
Sparse Core Ops, SparseCore 0:
  66.4 129.2 all-reduce.1
where the time goes:
time: 210 us
  waiting for transfers between devices  129 us (61%)
  blocking collectives  43.5 us (21%)
  between operations  15.4 us (7%)
  matrix products  9.97 us (5%)
  other arithmetic  9.29 us (4%)
  local copies, waits for them, and re-layouts  2.82 us (1%)
    psum x1, waiting for transfers between devices, on_device(): lax.psum(lax.dot_general(p_round, shard, (((0,), (0,)), ((), ())), prefer...  129 us
    psum x1, blocking collectives, on_device(): lax.psum(jnp.dot(p_sum.T, p_sum, precision=lax.Precision.HIGHEST), 'fsdp')  26 us
    psum x1, blocking collectives, on_device(): p_sum = lax.psum(local_p, 'rep')  17.5 us
  transfers between devices with their start and end apart: 1, of which 1 were waited for; matrix products, arithmetic and copies ran while one was open for 0% of the time, Pallas kernels for 0%

commit v1 on v0

--- a/solution.py
+++ b/solution.py
@@ -3,7 +3,296 @@
 import jax
 import jax.numpy as jnp
 from jax import lax
+from jax.experimental import pallas as pl
+from jax.experimental.pallas import tpu as pltpu
 from jax.sharding import PartitionSpec as P
+
+
+MESH = pl.DeviceIdType.MESH
+F32 = jnp.float32
+BF16 = jnp.bfloat16
+REPS = 4
+FSDP = 8
+CHIPS = 4
+RANK = 32
+HALF = 16
+FLIPS = ((1, 1), (0, 1), (1, 0), (0, 0))
+
+
+def round_kernel(
+    acc_hbm, startq_hbm, max_rms, update_ref, nextq_ref,
+    shard, startq, p_all, g_all, own_q, core_out, core_in, rep_out, rep_in,
+    total, z_out, z_in, gathered, final, final_in, norms, product,
+    load_sem, loadq_sem, p_send, p_recv, g_send, g_recv, core_send, core_recv,
+    rep_send, rep_recv, z_send, z_recv, ag_send, ag_recv, relay_send, relay_recv,
+    fin_send, fin_recv, norm_send, norm_recv,
+):
+    rep = lax.axis_index("rep")
+    fsdp = lax.axis_index("fsdp")
+    z, core = fsdp // 2, fsdp % 2
+    y, x = rep // 2, rep % 2
+    block = shard.shape[2]
+    piece = block // CHIPS
+    elements = shard.shape[1] * FSDP * block * REPS
+    reps = [((y + dy) % 2) * 2 + (x + dx) % 2 for dy, dx in FLIPS]
+    partner = z * 2 + (core + 1) % 2
+
+    def remote(src, dst, send, recv, to_rep, to_fsdp):
+        copy = pltpu.make_async_remote_copy(
+            src_ref=src, dst_ref=dst, send_sem=send, recv_sem=recv,
+            device_id=(to_rep, to_fsdp), device_id_type=MESH,
+        )
+        copy.start()
+        return copy
+
+    loads = []
+    for c in range(REPS):
+        columns = pl.ds(c * block, block)
+        first = pltpu.make_async_copy(startq_hbm.at[:, columns], startq.at[c], loadq_sem.at[c])
+        second = pltpu.make_async_copy(acc_hbm.at[0, :, columns], shard.at[c], load_sem.at[c])
+        first.start()
+        second.start()
+        loads.append((first, second))
+
+    barrier = pltpu.get_barrier_semaphore()
+    for s in range(REPS - 1):
+        pl.semaphore_signal(barrier, inc=1, device_id=(reps[s], fsdp), device_id_type=MESH)
+    for d in range(1, FSDP):
+        pl.semaphore_signal(
+            barrier, inc=1, device_id=(rep, (fsdp + d) % FSDP), device_id_type=MESH
+        )
+
+    local_p = jnp.zeros((RANK, shard.shape[1]), F32)
+    for c in range(REPS):
+        for load in loads[c]:
+            load.wait()
+        local_p += lax.dot_general(
+            startq[c], shard[c], (((1,), (1,)), ((), ())), preferred_element_type=F32
+        )
+    p_all[rep] = local_p
+    pl.semaphore_wait(barrier, REPS - 1 + FSDP - 1)
+
+    copies = [
+        remote(p_all.at[rep], p_all.at[rep], p_send.at[s], p_recv.at[s], reps[s], fsdp)
+        for s in range(REPS - 1)
+    ]
+    for copy in copies:
+        copy.wait_recv()
+    p_sum = p_all[0] + p_all[1] + p_all[2] + p_all[3]
+    padded = jnp.concatenate([p_sum, jnp.zeros((128 - RANK, p_sum.shape[1]), F32)], axis=0)
+    g_all[fsdp] = lax.dot_general(
+        p_sum, padded, (((1,), (1,)), ((), ())),
+        precision=lax.Precision.HIGHEST, preferred_element_type=F32,
+    )
+    sends = list(copies)
+    copies = [
+        remote(
+            g_all.at[fsdp], g_all.at[fsdp], g_send.at[d - 1], g_recv.at[d - 1],
+            rep, (fsdp + d) % FSDP,
+        )
+        for d in range(1, FSDP)
+    ]
+    for copy in copies:
+        copy.wait_recv()
+    sends += copies
+    gram = g_all[0]
+    for i in range(1, FSDP):
+        gram = gram + g_all[i]
+
+    g = [gram[8 * t : 8 * t + 8] for t in range(RANK // 8)]
+    p = [p_sum[8 * t : 8 * t + 8] for t in range(RANK // 8)]
+    line = lax.broadcasted_iota(jnp.int32, (8, 128), 0)
+    pivots = [jnp.ones((8, 128), F32) for _ in g]
+    for k in range(RANK):
+        t, r = k // 8, k % 8
+        row_g, row_p = g[t][r : r + 1], p[t][r : r + 1]
+        pivot = row_g[:, k : k + 1]
+        pivots[t] = jnp.where(line == r, pivot, pivots[t])
+        inverse = 1.0 / pivot
+        row_g, row_p = row_g * inverse, row_p * inverse
+        for u in range(t, RANK // 8):
+            factor = jnp.broadcast_to(g[u][:, k : k + 1], (8, 128))
+            if u == t:
+                factor = jnp.where(line > r, factor, 0.0)
+            g[u] = g[u] - factor * row_g
+            p[u] = p[u] - factor * row_p
+    p_hat = [p[t] * lax.rsqrt(pivots[t]) for t in range(RANK // 8)]
+    p_round = jnp.concatenate(p_hat, axis=0).astype(BF16)
+    lower_half = jnp.concatenate(p_hat[:2], axis=0)
+    upper_half = jnp.concatenate(p_hat[2:], axis=0)
+    is_first = core == 0
+    own_first = jnp.concatenate(
+        [jnp.where(is_first, lower_half, upper_half), jnp.where(is_first, upper_half, lower_half)],
+        axis=0,
+    ).astype(BF16)
+
+    core_copies, rep_copies = [], []
+
+    def to_replica(s):
+        core_copies[s].wait_recv()
+        summed = own_q[s] + core_in[s].astype(F32)
+        if s < REPS - 1:
+            rep_out[s] = summed.astype(BF16)
+            rep_copies.append(
+                remote(
+                    rep_out.at[s], rep_in.at[s], rep_send.at[s], rep_recv.at[s], reps[s], fsdp
+                )
+            )
+        else:
+            own_q[s] = summed
+
+    for s in range(REPS):
+        terms = jnp.dot(own_first, shard[reps[s]], preferred_element_type=F32)
+        own_q[s] = terms[:HALF]
+        core_out[s] = terms[HALF:].astype(BF16)
+        core_copies.append(
+            remote(
+                core_out.at[s], core_in.at[s], core_send.at[s], core_recv.at[s], rep, partner
+            )
+        )
+        if s > 0:
+            to_replica(s - 1)
+    to_replica(REPS - 1)
+    sends += core_copies + rep_copies
+
+    for copy in rep_copies:
+        copy.wait_recv()
+    for q in range(CHIPS):
+        columns = pl.ds(q * piece, piece)
+        value = own_q[REPS - 1, :, columns]
+        for s in range(REPS - 1):
+            value = value + rep_in[s, :, columns].astype(F32)
+        total[q] = value
+    z_copies = []
+    for d in (2, 1, 3):
+        to = (z + d) % CHIPS
+        z_out[d - 1] = total[to].astype(BF16)
+        z_copies.append(
+            remote(
+                z_out.at[d - 1], z_in.at[d - 1], z_send.at[d - 1], z_recv.at[d - 1],
+                rep, to * 2 + core,
+            )
+        )
+    for copy in z_copies:
+        copy.wait_recv()
+    sends += z_copies
+    mine = total[z] + z_in[0].astype(F32) + z_in[1].astype(F32) + z_in[2].astype(F32)
+    final[...] = mine
+    gathered[core, z] = mine.astype(BF16)
+    ag_copies = []
+    for d in (2, 1, 3):
+        ag_copies.append(
+            remote(
+                gathered.at[core, z], gathered.at[core, z], ag_send.at[d - 1],
+                ag_recv.at[d - 1], rep, ((z + d) % CHIPS) * 2 + core,
+            )
+        )
+    relays = [
+        remote(
+            gathered.at[core, z], gathered.at[core, z], relay_send.at[0], relay_recv.at[0],
+            rep, partner,
+        )
+    ]
+    fin_copy = remote(final, final_in, fin_send, fin_recv, rep, partner)
+    for copy, d in zip(ag_copies, (2, 1, 3)):
+        copy.wait_recv()
+        source = (z + CHIPS - d) % CHIPS
+        relays.append(
+            remote(
+                gathered.at[core, source], gathered.at[core, source], relay_send.at[d],
+                relay_recv.at[d], rep, partner,
+            )
+        )
+    nextq_ref[pl.ds(pl.multiple_of(core * HALF, HALF), HALF), :] = mine
+    fin_copy.wait_recv()
+    nextq_ref[pl.ds(pl.multiple_of((1 - core) * HALF, HALF), HALF), :] = final_in[...]
+    for copy in relays:
+        copy.wait_recv()
+    sends += ag_copies + relays + [fin_copy]
+
+    squares = jnp.zeros((1, piece), F32)
+    for q in range(CHIPS):
+        for h in range(2):
+            value = gathered[h, q].astype(F32)
+            squares = squares + jnp.sum(value * value, axis=0, keepdims=True)
+    norms[rep] = jnp.broadcast_to(jnp.sum(squares, axis=1, keepdims=True), (8, 128))
+    copies = [
+        remote(norms.at[rep], norms.at[rep], norm_send.at[s], norm_recv.at[s], reps[s], fsdp)
+        for s in range(REPS - 1)
+    ]
+    sends += copies
+    for q in range(CHIPS):
+        right = jnp.concatenate([gathered[0, q], gathered[1, q]], axis=0)
+        product[q] = lax.dot_general(
+            p_round, right, (((0,), (0,)), ((), ())), preferred_element_type=F32
+        )
+    for copy in copies:
+        copy.wait_recv()
+    norm_sq = (norms[0] + norms[1] + norms[2] + norms[3])[:1, :1]
+    limit = max_rms[0] * math.sqrt(elements)
+    scale = jnp.minimum(1.0, limit / jnp.sqrt(norm_sq))
+    for q in range(CHIPS):
+        update_ref[:, pl.ds(q * piece, piece)] = (scale * product[q]).astype(BF16)
+    for copy in sends:
+        copy.wait_send()
+
+
+def on_block(accumulated, start_q, max_rms):
+    rows, width = accumulated.shape[1:]
+    block = width // REPS
+    piece = block // CHIPS
+    dma = pltpu.SemaphoreType.DMA
+    update, chip_q = pl.pallas_call(
+        round_kernel,
+        out_shape=(
+            jax.ShapeDtypeStruct((rows, block), BF16),
+            jax.ShapeDtypeStruct((RANK, piece), F32),
+        ),
+        in_specs=[
+            pl.BlockSpec(memory_space=pl.ANY),
+            pl.BlockSpec(memory_space=pl.ANY),
+            pl.BlockSpec(memory_space=pltpu.SMEM),
+        ],
+        out_specs=(
+            pl.BlockSpec(memory_space=pltpu.VMEM),
+            pl.BlockSpec(memory_space=pltpu.VMEM),
+        ),
+        scratch_shapes=[
+            pltpu.VMEM((REPS, rows, block), BF16),
+            pltpu.VMEM((REPS, RANK, block), BF16),
+            pltpu.VMEM((REPS, RANK, rows), F32),
+            pltpu.VMEM((FSDP, RANK, 128), F32),
+            pltpu.VMEM((REPS, HALF, block), F32),
+            pltpu.VMEM((REPS, HALF, block), BF16),
+            pltpu.VMEM((REPS, HALF, block), BF16),
+            pltpu.VMEM((REPS - 1, HALF, block), BF16),
+            pltpu.VMEM((REPS - 1, HALF, block), BF16),
+            pltpu.VMEM((CHIPS, HALF, piece), F32),
+            pltpu.VMEM((CHIPS - 1, HALF, piece), BF16),
+            pltpu.VMEM((CHIPS - 1, HALF, piece), BF16),
+            pltpu.VMEM((2, CHIPS, HALF, piece), BF16),
+            pltpu.VMEM((HALF, piece), F32),
+            pltpu.VMEM((HALF, piece), F32),
+            pltpu.VMEM((REPS, 8, 128), F32),
+            pltpu.VMEM((CHIPS, rows, piece), F32),
+            dma((REPS,)), dma((REPS,)),
+            dma((REPS - 1,)), dma((REPS - 1,)),
+            dma((FSDP - 1,)), dma((FSDP - 1,)),
+            dma((REPS,)), dma((REPS,)),
+            dma((REPS - 1,)), dma((REPS - 1,)),
+            dma((CHIPS - 1,)), dma((CHIPS - 1,)),
+            dma((CHIPS - 1,)), dma((CHIPS - 1,)),
+            dma((CHIPS,)), dma((CHIPS,)),
+            dma, dma,
+            dma((REPS - 1,)), dma((REPS - 1,)),
+        ],
+        compiler_params=pltpu.CompilerParams(
+            collective_id=0, has_side_effects=True, vmem_limit_bytes=40 * 1024 * 1024
+        ),
+    )(accumulated, start_q, max_rms)
+    own = piece // 2
+    next_q = lax.dynamic_slice_in_dim(chip_q, (lax.axis_index("fsdp") % 2) * own, own, 1)
+    return (update, next_q)
 
 
 def orthonormal(part_rows, gram):
@@ -48,8 +337,9 @@
 
 
 def solution(mesh):
+    fits = mesh.shape["rep"] == REPS and mesh.shape["fsdp"] == FSDP
     return jax.shard_map(
-        on_device,
+        on_block if fits else on_device,
         mesh=mesh,
         in_specs=(P("rep", "fsdp", None), P(), P()),
         out_specs=(P("fsdp", "rep"), P(None, ("rep", "fsdp"))),

time: 210 us -> 44.6 us (0.21)
  waiting for transfers between devices: 129 us -> 0 us
  blocking collectives: 43.5 us -> 0 us
  Pallas kernels: 0 us -> 38.2 us
  between operations: 15.4 us -> 1.31 us
  matrix products: 9.97 us -> 0 us
  other arithmetic: 9.29 us -> 0 us
    psum x1 -> x0, waiting for transfers between devices: 129 us -> none  [on_device(): lax.psum(lax.dot_general(p_round, shard, (((0,), (0,)), ((), ())), prefer...]
    psum x2 -> x0, blocking collectives: 43.5 us -> none  [the longest x1 26 us: on_device(): lax.psum(jnp.dot(p_sum.T, p_sum, precision=lax.Precision.HIGHEST), 'fsdp')]
    pallas_call x0 -> x1, Pallas kernels: none -> 38.2 us  [on_block(): pl.pallas_call(round_kernel, out_shape=(jax.ShapeDtypeStruct((rows, block...]
    dot_general x4 -> x0, matrix products: 9.75 us -> none  [the longest x1 3.89 us: on_device(): lax.dot_general(p_round, shard, (((0,), (0,)), ((), ())), preferred_eleme...]
    another operation x5 -> x0, other arithmetic: 6.71 us -> none  [the longest x3 3.59 us: orthonormal(): lower = jnp.linalg.cholesky(gram)]
    unnamed x2 -> x5, local copies, waits for them, and re-layouts: 1.13 us -> 4.13 us
    reduce_sum x1 -> x0, other arithmetic: 2.57 us -> none  [on_device(): norm_sq = jnp.sum(q_full * q_full)]
  transfers between devices with their start and end apart: 1 -> 0, of which waited for: 1 -> 0; matrix products, arithmetic and copies ran while one was open for 0% -> 0% of each run, Pallas kernels for 0% -> 0%
where the time goes in v1:
time: 44.6 us; the launch traced here: 44.4 us
  Pallas kernels  38.2 us (86%)
  local copies, waits for them, and re-layouts  4.85 us (11%)
  between operations  1.31 us (3%)
    pallas_call x1, Pallas kernels, on_block(): pl.pallas_call(round_kernel, out_shape=(jax.ShapeDtypeStruct((rows, block...  38.2 us
    unnamed x5, local copies, waits for them, and re-layouts  4.13 us

profile of v1, /device:TPU:0, one launch (start us, length us, event | category | flops | bytes accessed | tf_op | source)
XLA Modules:
  0.0 44.4 jit_solution(10175028847712641985)
XLA Ops:
  1.3 0.0 copy-start
  1.3 2.0 %copy-done = bf16[1,128,14336]{2,1,0:T(8,128)(2,1)S(1)} copy-done((bf16[1,128,14336]{2,1,0:T(8,128)(2,1)S(1)}, bf16[1,128,14336]{2,1,0:T(8,128)(2,1)}, u32[]{:S(2)}) %copy-start) | copy-done | bytes 3670040
  3.3 0.0 copy-start.1
  3.3 1.2 %copy-done.1 = bf16[32,14336]{1,0:T(8,128)(2,1)S(1)} copy-done((bf16[32,14336]{1,0:T(8,128)(2,1)S(1)}, bf16[32,14336]{1,0:T(8,128)(2,1)}, u32[]{:S(2)}) %copy-start.1) | copy-done | bytes 917528
  4.5 38.2 %shard_map.50 = (bf16[128,3584]{1,0:T(8,128)(2,1)S(1)}, f32[32,896]{1,0:T(8,128)S(1)}) custom-call(bf16[1,128,14336]{2,1,0:T(8,128)(2,1)S(1)} %copy-done, bf16[32,14336]{1,0:T(8,128)(2,1)S(1)} %copy-done.1, f32[1]{0:T(128)S(6)} %copy.6.max_rms), custom_call_target="tpu_custom_call" | custom-call | tf_op jit(solution)/shard_map/pallas_call | solution.py:245
  42.7 0.7 %constant_dynamic-slice_fusion = f32[32,448]{1,0:T(8,128)} fusion(f32[32,896]{1,0:T(8,128)S(1)} %get-tuple-element.5, s32[]{:T(128)S(6)} %select_n.11), kind=kLoop, calls=%fused_computation | loop fusion | bytes 114692 | tf_op jit(solution)/shard_map/dynamic_slice | solution.py:294
  43.5 0.9 %copy.7 = bf16[128,3584]{1,0:T(8,128)(2,1)} copy(bf16[128,3584]{1,0:T(8,128)(2,1)S(1)} %get-tuple-element.8) | data formatting | bytes 1835008
Async XLA Ops:
  1.3 2.0 %copy-start = (bf16[1,128,14336]{2,1,0:T(8,128)(2,1)S(1)}, bf16[1,128,14336]{2,1,0:T(8,128)(2,1)}, u32[]{:S(2)}) copy-start(bf16[1,128,14336]{2,1,0:T(8,128)(2,1)} %acc_hbm.1) | copy-start | bytes 11010052
  3.3 1.2 %copy-start.1 = (bf16[32,14336]{1,0:T(8,128)(2,1)S(1)}, bf16[32,14336]{1,0:T(8,128)(2,1)}, u32[]{:S(2)}) copy-start(bf16[32,14336]{1,0:T(8,128)(2,1)} %startq_hbm.1) | copy-start | bytes 2752516

commit v2 on v1

--- a/solution.py
+++ b/solution.py
@@ -16,16 +16,18 @@
 CHIPS = 4
 RANK = 32
 HALF = 16
+AWAY = (2, 1, 3)
+LAG = 4
 FLIPS = ((1, 1), (0, 1), (1, 0), (0, 0))
 
 
 def round_kernel(
     acc_hbm, startq_hbm, max_rms, update_ref, nextq_ref,
     shard, startq, p_all, g_all, own_q, core_out, core_in, rep_out, rep_in,
-    total, z_out, z_in, gathered, final, final_in, norms, product,
+    total, z_out, z_in, gathered, final, final_in, norms, all_norms,
     load_sem, loadq_sem, p_send, p_recv, g_send, g_recv, core_send, core_recv,
     rep_send, rep_recv, z_send, z_recv, ag_send, ag_recv, relay_send, relay_recv,
-    fin_send, fin_recv, norm_send, norm_recv,
+    fin_send, fin_recv, norm_send, norm_recv, all_send, all_recv,
 ):
     rep = lax.axis_index("rep")
     fsdp = lax.axis_index("fsdp")
@@ -71,6 +73,7 @@
         )
     p_all[rep] = local_p
     pl.semaphore_wait(barrier, REPS - 1 + FSDP - 1)
+    sends = []
 
     copies = [
         remote(p_all.at[rep], p_all.at[rep], p_send.at[s], p_recv.at[s], reps[s], fsdp)
@@ -84,7 +87,7 @@
         p_sum, padded, (((1,), (1,)), ((), ())),
         precision=lax.Precision.HIGHEST, preferred_element_type=F32,
     )
-    sends = list(copies)
+    sends += copies
     copies = [
         remote(
             g_all.at[fsdp], g_all.at[fsdp], g_send.at[d - 1], g_recv.at[d - 1],
@@ -126,113 +129,119 @@
         axis=0,
     ).astype(BF16)
 
-    core_copies, rep_copies = [], []
-
-    def to_replica(s):
-        core_copies[s].wait_recv()
-        summed = own_q[s] + core_in[s].astype(F32)
+    quarters = [(z + d) % CHIPS for d in AWAY + (0,)]
+    pieces = [(i, s) for i in range(CHIPS) for s in range(REPS - 1)]
+    pieces += [(i, REPS - 1) for i in range(CHIPS)]
+    core_copies, rep_copies = [], {}
+
+    def to_replica(n):
+        i, s = pieces[n]
+        core_copies[n].wait_recv()
+        summed = own_q[n] + core_in[n].astype(F32)
         if s < REPS - 1:
-            rep_out[s] = summed.astype(BF16)
-            rep_copies.append(
+            rep_out[n] = summed.astype(BF16)
+            rep_copies[i, s] = remote(
+                rep_out.at[n], rep_in.at[n], rep_send.at[n], rep_recv.at[n], reps[s], fsdp
+            )
+        else:
+            total[i] = summed
+
+    for n, (i, s) in enumerate(pieces):
+        columns = pl.ds(pl.multiple_of(quarters[i] * piece, 128), piece)
+        terms = jnp.dot(own_first, shard[reps[s], :, columns], preferred_element_type=F32)
+        own_q[n] = terms[:HALF]
+        core_out[n] = terms[HALF:].astype(BF16)
+        core_copies.append(
+            remote(
+                core_out.at[n], core_in.at[n], core_send.at[n], core_recv.at[n], rep, partner
+            )
+        )
+        if n >= LAG:
+            to_replica(n - LAG)
+    for n in range(len(pieces) - LAG, len(pieces)):
+        to_replica(n)
+    sends += core_copies + list(rep_copies.values())
+
+    z_copies = []
+    for i in range(CHIPS):
+        value = total[i]
+        for s in range(REPS - 1):
+            rep_copies[i, s].wait_recv()
+            value = value + rep_in[pieces.index((i, s))].astype(F32)
+        if i < CHIPS - 1:
+            z_out[i] = value.astype(BF16)
+            z_copies.append(
                 remote(
-                    rep_out.at[s], rep_in.at[s], rep_send.at[s], rep_recv.at[s], reps[s], fsdp
+                    z_out.at[i], z_in.at[i], z_send.at[i], z_recv.at[i],
+                    rep, quarters[i] * 2 + core,
                 )
             )
         else:
-            own_q[s] = summed
-
-    for s in range(REPS):
-        terms = jnp.dot(own_first, shard[reps[s]], preferred_element_type=F32)
-        own_q[s] = terms[:HALF]
-        core_out[s] = terms[HALF:].astype(BF16)
-        core_copies.append(
-            remote(
-                core_out.at[s], core_in.at[s], core_send.at[s], core_recv.at[s], rep, partner
-            )
-        )
-        if s > 0:
-            to_replica(s - 1)
-    to_replica(REPS - 1)
-    sends += core_copies + rep_copies
-
-    for copy in rep_copies:
-        copy.wait_recv()
-    for q in range(CHIPS):
-        columns = pl.ds(q * piece, piece)
-        value = own_q[REPS - 1, :, columns]
-        for s in range(REPS - 1):
-            value = value + rep_in[s, :, columns].astype(F32)
-        total[q] = value
-    z_copies = []
-    for d in (2, 1, 3):
-        to = (z + d) % CHIPS
-        z_out[d - 1] = total[to].astype(BF16)
-        z_copies.append(
-            remote(
-                z_out.at[d - 1], z_in.at[d - 1], z_send.at[d - 1], z_recv.at[d - 1],
-                rep, to * 2 + core,
-            )
-        )
-    for copy in z_copies:
-        copy.wait_recv()
+            mine = value
     sends += z_copies
-    mine = total[z] + z_in[0].astype(F32) + z_in[1].astype(F32) + z_in[2].astype(F32)
+    for copy, i in zip(z_copies, range(CHIPS - 1)):
+        copy.wait_recv()
+        mine = mine + z_in[i].astype(F32)
     final[...] = mine
     gathered[core, z] = mine.astype(BF16)
-    ag_copies = []
-    for d in (2, 1, 3):
-        ag_copies.append(
-            remote(
-                gathered.at[core, z], gathered.at[core, z], ag_send.at[d - 1],
-                ag_recv.at[d - 1], rep, ((z + d) % CHIPS) * 2 + core,
-            )
-        )
+    ag_copies = [
+        remote(
+            gathered.at[core, z], gathered.at[core, z], ag_send.at[i], ag_recv.at[i],
+            rep, quarters[i] * 2 + core,
+        )
+        for i in range(CHIPS - 1)
+    ]
     relays = [
         remote(
-            gathered.at[core, z], gathered.at[core, z], relay_send.at[0], relay_recv.at[0],
-            rep, partner,
+            gathered.at[core, z], gathered.at[core, z], relay_send.at[CHIPS - 1],
+            relay_recv.at[CHIPS - 1], rep, partner,
         )
     ]
     fin_copy = remote(final, final_in, fin_send, fin_recv, rep, partner)
-    for copy, d in zip(ag_copies, (2, 1, 3)):
-        copy.wait_recv()
-        source = (z + CHIPS - d) % CHIPS
+    squares = jnp.sum(jnp.sum(mine * mine, axis=0, keepdims=True), axis=1, keepdims=True)
+    norms[rep] = jnp.broadcast_to(squares, (8, 128))
+    norm_copies = [
+        remote(norms.at[rep], norms.at[rep], norm_send.at[s], norm_recv.at[s], reps[s], fsdp)
+        for s in range(REPS - 1)
+    ]
+    nextq_ref[pl.ds(pl.multiple_of(core * HALF, HALF), HALF), :] = mine
+    for copy in norm_copies:
+        copy.wait_recv()
+    all_norms[fsdp] = norms[0] + norms[1] + norms[2] + norms[3]
+    all_copies = [
+        remote(
+            all_norms.at[fsdp], all_norms.at[fsdp], all_send.at[d - 1], all_recv.at[d - 1],
+            rep, (fsdp + d) % FSDP,
+        )
+        for d in range(1, FSDP)
+    ]
+    sources = [(z + CHIPS - d) % CHIPS for d in AWAY] + [z]
+    for i in range(CHIPS - 1):
+        ag_copies[i].wait_recv()
         relays.append(
             remote(
-                gathered.at[core, source], gathered.at[core, source], relay_send.at[d],
-                relay_recv.at[d], rep, partner,
+                gathered.at[core, sources[i]], gathered.at[core, sources[i]],
+                relay_send.at[i], relay_recv.at[i], rep, partner,
             )
         )
-    nextq_ref[pl.ds(pl.multiple_of(core * HALF, HALF), HALF), :] = mine
     fin_copy.wait_recv()
     nextq_ref[pl.ds(pl.multiple_of((1 - core) * HALF, HALF), HALF), :] = final_in[...]
-    for copy in relays:
-        copy.wait_recv()
-    sends += ag_copies + relays + [fin_copy]
-
-    squares = jnp.zeros((1, piece), F32)
-    for q in range(CHIPS):
-        for h in range(2):
-            value = gathered[h, q].astype(F32)
-            squares = squares + jnp.sum(value * value, axis=0, keepdims=True)
-    norms[rep] = jnp.broadcast_to(jnp.sum(squares, axis=1, keepdims=True), (8, 128))
-    copies = [
-        remote(norms.at[rep], norms.at[rep], norm_send.at[s], norm_recv.at[s], reps[s], fsdp)
-        for s in range(REPS - 1)
-    ]
-    sends += copies
-    for q in range(CHIPS):
+    for copy in all_copies:
+        copy.wait_recv()
+    norm_sq = all_norms[0]
+    for i in range(1, FSDP):
+        norm_sq = norm_sq + all_norms[i]
+    sends += ag_copies + relays + [fin_copy] + norm_copies + all_copies
+    limit = max_rms[0] * math.sqrt(elements)
+    scale = jnp.minimum(1.0, limit / jnp.sqrt(norm_sq[:1, :1]))
+    for copy, q in zip(relays, sources[-1:] + sources[:-1]):
+        copy.wait_recv()
         right = jnp.concatenate([gathered[0, q], gathered[1, q]], axis=0)
-        product[q] = lax.dot_general(
+        product = lax.dot_general(
             p_round, right, (((0,), (0,)), ((), ())), preferred_element_type=F32
         )
-    for copy in copies:
-        copy.wait_recv()
-    norm_sq = (norms[0] + norms[1] + norms[2] + norms[3])[:1, :1]
-    limit = max_rms[0] * math.sqrt(elements)
-    scale = jnp.minimum(1.0, limit / jnp.sqrt(norm_sq))
-    for q in range(CHIPS):
-        update_ref[:, pl.ds(q * piece, piece)] = (scale * product[q]).astype(BF16)
+        columns = pl.ds(pl.multiple_of(q * piece, 128), piece)
+        update_ref[:, columns] = (scale * product).astype(BF16)
     for copy in sends:
         copy.wait_send()
 
@@ -249,8 +258,8 @@
             jax.ShapeDtypeStruct((RANK, piece), F32),
         ),
         in_specs=[
-            pl.BlockSpec(memory_space=pl.ANY),
-            pl.BlockSpec(memory_space=pl.ANY),
+            pl.BlockSpec(memory_space=pltpu.HBM),
+            pl.BlockSpec(memory_space=pltpu.HBM),
             pl.BlockSpec(memory_space=pltpu.SMEM),
         ],
         out_specs=(
@@ -262,11 +271,11 @@
             pltpu.VMEM((REPS, RANK, block), BF16),
             pltpu.VMEM((REPS, RANK, rows), F32),
             pltpu.VMEM((FSDP, RANK, 128), F32),
-            pltpu.VMEM((REPS, HALF, block), F32),
-            pltpu.VMEM((REPS, HALF, block), BF16),
-            pltpu.VMEM((REPS, HALF, block), BF16),
-            pltpu.VMEM((REPS - 1, HALF, block), BF16),
-            pltpu.VMEM((REPS - 1, HALF, block), BF16),
+            pltpu.VMEM((REPS * CHIPS, HALF, piece), F32),
+            pltpu.VMEM((REPS * CHIPS, HALF, piece), BF16),
+            pltpu.VMEM((REPS * CHIPS, HALF, piece), BF16),
+            pltpu.VMEM(((REPS - 1) * CHIPS, HALF, piece), BF16),
+            pltpu.VMEM(((REPS - 1) * CHIPS, HALF, piece), BF16),
             pltpu.VMEM((CHIPS, HALF, piece), F32),
             pltpu.VMEM((CHIPS - 1, HALF, piece), BF16),
             pltpu.VMEM((CHIPS - 1, HALF, piece), BF16),
@@ -274,17 +283,18 @@
             pltpu.VMEM((HALF, piece), F32),
             pltpu.VMEM((HALF, piece), F32),
             pltpu.VMEM((REPS, 8, 128), F32),
-            pltpu.VMEM((CHIPS, rows, piece), F32),
+            pltpu.VMEM((FSDP, 8, 128), F32),
             dma((REPS,)), dma((REPS,)),
             dma((REPS - 1,)), dma((REPS - 1,)),
             dma((FSDP - 1,)), dma((FSDP - 1,)),
-            dma((REPS,)), dma((REPS,)),
-            dma((REPS - 1,)), dma((REPS - 1,)),
+            dma((REPS * CHIPS,)), dma((REPS * CHIPS,)),
+            dma(((REPS - 1) * CHIPS,)), dma(((REPS - 1) * CHIPS,)),
             dma((CHIPS - 1,)), dma((CHIPS - 1,)),
             dma((CHIPS - 1,)), dma((CHIPS - 1,)),
             dma((CHIPS,)), dma((CHIPS,)),
             dma, dma,
             dma((REPS - 1,)), dma((REPS - 1,)),
+            dma((FSDP - 1,)), dma((FSDP - 1,)),
         ],
         compiler_params=pltpu.CompilerParams(
             collective_id=0, has_side_effects=True, vmem_limit_bytes=40 * 1024 * 1024

time: 44.6 us -> 42.6 us (0.955)
  Pallas kernels: 38.2 us -> 36.3 us
    pallas_call x1, Pallas kernels: 38.2 us -> 36.3 us  [on_block(): pl.pallas_call(round_kernel, out_shape=(jax.ShapeDtypeStruct((rows, block...]
where the time goes in v2:
time: 42.6 us; the launch traced here: 42.4 us
  Pallas kernels  36.3 us (85%)
  local copies, waits for them, and re-layouts  4.85 us (11%)
  between operations  1.31 us (3%)
    pallas_call x1, Pallas kernels, on_block(): pl.pallas_call(round_kernel, out_shape=(jax.ShapeDtypeStruct((rows, block...  36.3 us
    unnamed x5, local copies, waits for them, and re-layouts  4.13 us

profile of v2, /device:TPU:0, one launch (start us, length us, event | category | flops | bytes accessed | tf_op | source)
XLA Modules:
  0.0 42.4 jit_solution(14636507821942078831)
XLA Ops:
  1.3 0.0 copy-start
  1.3 2.0 %copy-done = bf16[1,128,14336]{2,1,0:T(8,128)(2,1)S(1)} copy-done((bf16[1,128,14336]{2,1,0:T(8,128)(2,1)S(1)}, bf16[1,128,14336]{2,1,0:T(8,128)(2,1)}, u32[]{:S(2)}) %copy-start) | copy-done | bytes 3670040
  3.3 0.0 copy-start.1
  3.3 1.2 %copy-done.1 = bf16[32,14336]{1,0:T(8,128)(2,1)S(1)} copy-done((bf16[32,14336]{1,0:T(8,128)(2,1)S(1)}, bf16[32,14336]{1,0:T(8,128)(2,1)}, u32[]{:S(2)}) %copy-start.1) | copy-done | bytes 917528
  4.5 36.3 %shard_map.50 = (bf16[128,3584]{1,0:T(8,128)(2,1)S(1)}, f32[32,896]{1,0:T(8,128)S(1)}) custom-call(bf16[1,128,14336]{2,1,0:T(8,128)(2,1)S(1)} %copy-done, bf16[32,14336]{1,0:T(8,128)(2,1)S(1)} %copy-done.1, f32[1]{0:T(128)S(6)} %copy.6.max_rms), custom_call_target="tpu_custom_call" | custom-call | tf_op jit(solution)/shard_map/pallas_call | solution.py:254
  40.8 0.7 %constant_dynamic-slice_fusion = f32[32,448]{1,0:T(8,128)} fusion(f32[32,896]{1,0:T(8,128)S(1)} %get-tuple-element.5, s32[]{:T(128)S(6)} %select_n.11), kind=kLoop, calls=%fused_computation | loop fusion | bytes 114692 | tf_op jit(solution)/shard_map/dynamic_slice | solution.py:304
  41.5 0.9 %copy.7 = bf16[128,3584]{1,0:T(8,128)(2,1)} copy(bf16[128,3584]{1,0:T(8,128)(2,1)S(1)} %get-tuple-element.8) | data formatting | bytes 1835008
Async XLA Ops:
  1.3 2.0 %copy-start = (bf16[1,128,14336]{2,1,0:T(8,128)(2,1)S(1)}, bf16[1,128,14336]{2,1,0:T(8,128)(2,1)}, u32[]{:S(2)}) copy-start(bf16[1,128,14336]{2,1,0:T(8,128)(2,1)} %acc_hbm.1) | copy-start | bytes 11010052
  3.3 1.2 %copy-start.1 = (bf16[32,14336]{1,0:T(8,128)(2,1)S(1)}, bf16[32,14336]{1,0:T(8,128)(2,1)}, u32[]{:S(2)}) copy-start(bf16[32,14336]{1,0:T(8,128)(2,1)} %startq_hbm.1) | copy-start | bytes 2752516

commit v3 on v2

--- a/solution.py
+++ b/solution.py
@@ -24,7 +24,7 @@
 def round_kernel(
     acc_hbm, startq_hbm, max_rms, update_ref, nextq_ref,
     shard, startq, p_all, g_all, own_q, core_out, core_in, rep_out, rep_in,
-    total, z_out, z_in, gathered, final, final_in, norms, all_norms,
+    total, z_out, z_in, gathered, final, final_in, norms, all_norms, products,
     load_sem, loadq_sem, p_send, p_recv, g_send, g_recv, core_send, core_recv,
     rep_send, rep_recv, z_send, z_recv, ag_send, ag_recv, relay_send, relay_recv,
     fin_send, fin_recv, norm_send, norm_recv, all_send, all_recv,
@@ -226,22 +226,22 @@
         )
     fin_copy.wait_recv()
     nextq_ref[pl.ds(pl.multiple_of((1 - core) * HALF, HALF), HALF), :] = final_in[...]
+    sends += ag_copies + relays + [fin_copy] + norm_copies + all_copies
+    for copy, q in zip(relays, sources[-1:] + sources[:-1]):
+        copy.wait_recv()
+        right = jnp.concatenate([gathered[0, q], gathered[1, q]], axis=0)
+        products[q] = lax.dot_general(
+            p_round, right, (((0,), (0,)), ((), ())), preferred_element_type=F32
+        )
     for copy in all_copies:
         copy.wait_recv()
     norm_sq = all_norms[0]
     for i in range(1, FSDP):
         norm_sq = norm_sq + all_norms[i]
-    sends += ag_copies + relays + [fin_copy] + norm_copies + all_copies
     limit = max_rms[0] * math.sqrt(elements)
     scale = jnp.minimum(1.0, limit / jnp.sqrt(norm_sq[:1, :1]))
-    for copy, q in zip(relays, sources[-1:] + sources[:-1]):
-        copy.wait_recv()
-        right = jnp.concatenate([gathered[0, q], gathered[1, q]], axis=0)
-        product = lax.dot_general(
-            p_round, right, (((0,), (0,)), ((), ())), preferred_element_type=F32
-        )
-        columns = pl.ds(pl.multiple_of(q * piece, 128), piece)
-        update_ref[:, columns] = (scale * product).astype(BF16)
+    for q in range(CHIPS):
+        update_ref[:, pl.ds(q * piece, piece)] = (scale * products[q]).astype(BF16)
     for copy in sends:
         copy.wait_send()
 
@@ -284,6 +284,7 @@
             pltpu.VMEM((HALF, piece), F32),
             pltpu.VMEM((REPS, 8, 128), F32),
             pltpu.VMEM((FSDP, 8, 128), F32),
+            pltpu.VMEM((CHIPS, rows, piece), F32),
             dma((REPS,)), dma((REPS,)),
             dma((REPS - 1,)), dma((REPS - 1,)),
             dma((FSDP - 1,)), dma((FSDP - 1,)),

time: 42.6 us -> 41.8 us (0.981)
  Pallas kernels: 36.3 us -> 35.4 us
    pallas_call x1, Pallas kernels: 36.3 us -> 35.4 us  [on_block(): pl.pallas_call(round_kernel, out_shape=(jax.ShapeDtypeStruct((rows, block...]
where the time goes in v3:
time: 41.8 us; the launch traced here: 41.6 us
  Pallas kernels  35.4 us (85%)
  local copies, waits for them, and re-layouts  4.85 us (12%)
  between operations  1.31 us (3%)
    pallas_call x1, Pallas kernels, on_block(): pl.pallas_call(round_kernel, out_shape=(jax.ShapeDtypeStruct((rows, block...  35.4 us
    unnamed x5, local copies, waits for them, and re-layouts  4.13 us

profile of v3, /device:TPU:0, one launch (start us, length us, event | category | flops | bytes accessed | tf_op | source)
XLA Modules:
  0.0 41.6 jit_solution(2799907068114753684)
XLA Ops:
  1.3 0.0 copy-start
  1.3 2.0 %copy-done = bf16[1,128,14336]{2,1,0:T(8,128)(2,1)S(1)} copy-done((bf16[1,128,14336]{2,1,0:T(8,128)(2,1)S(1)}, bf16[1,128,14336]{2,1,0:T(8,128)(2,1)}, u32[]{:S(2)}) %copy-start) | copy-done | bytes 3670040
  3.3 0.0 copy-start.1
  3.3 1.2 %copy-done.1 = bf16[32,14336]{1,0:T(8,128)(2,1)S(1)} copy-done((bf16[32,14336]{1,0:T(8,128)(2,1)S(1)}, bf16[32,14336]{1,0:T(8,128)(2,1)}, u32[]{:S(2)}) %copy-start.1) | copy-done | bytes 917528
  4.5 35.4 %shard_map.50 = (bf16[128,3584]{1,0:T(8,128)(2,1)S(1)}, f32[32,896]{1,0:T(8,128)S(1)}) custom-call(bf16[1,128,14336]{2,1,0:T(8,128)(2,1)S(1)} %copy-done, bf16[32,14336]{1,0:T(8,128)(2,1)S(1)} %copy-done.1, f32[1]{0:T(128)S(6)} %copy.6.max_rms), custom_call_target="tpu_custom_call" | custom-call | tf_op jit(solution)/shard_map/pallas_call | solution.py:254
  40.0 0.7 %constant_dynamic-slice_fusion = f32[32,448]{1,0:T(8,128)} fusion(f32[32,896]{1,0:T(8,128)S(1)} %get-tuple-element.5, s32[]{:T(128)S(6)} %select_n.11), kind=kLoop, calls=%fused_computation | loop fusion | bytes 114692 | tf_op jit(solution)/shard_map/dynamic_slice | solution.py:305
  40.7 0.9 %copy.7 = bf16[128,3584]{1,0:T(8,128)(2,1)} copy(bf16[128,3584]{1,0:T(8,128)(2,1)S(1)} %get-tuple-element.8) | data formatting | bytes 1835008
Async XLA Ops:
  1.3 2.0 %copy-start = (bf16[1,128,14336]{2,1,0:T(8,128)(2,1)S(1)}, bf16[1,128,14336]{2,1,0:T(8,128)(2,1)}, u32[]{:S(2)}) copy-start(bf16[1,128,14336]{2,1,0:T(8,128)(2,1)} %acc_hbm.1) | copy-start | bytes 11010052
  3.3 1.2 %copy-start.1 = (bf16[32,14336]{1,0:T(8,128)(2,1)S(1)}, bf16[32,14336]{1,0:T(8,128)(2,1)}, u32[]{:S(2)}) copy-start(bf16[32,14336]{1,0:T(8,128)(2,1)} %startq_hbm.1) | copy-start | bytes 2752516
